TPU v7x, 32 devices: a whole 2x2x4 slice. The times are simulated.
32 devices in a mesh: events: 2 (over x), shells: 16 (over z, y, core).
Axes of the slice: x: 2, y: 2, z: 4, core: 2. Of those that a mesh axis runs over, the one named last changes fastest.
Arguments:
- model: bfloat16 [1048576], P('shells'), may hold values from -6 to 6
- sensitivity: bfloat16 [16384, 64, 128], P(('events', 'shells')), may hold values from -0.1875 to 0.1875
- pick_block: int32 [16384], P(('events', 'shells')), may hold values from 0 to 1023, as said below
- cell_block: int32 [16384], P(('events', 'shells')), may hold values from 0 to 511
- blk_count: int32 [32], P(('events', 'shells')), may hold values from 128 to 512, as said below
- observed: float32 [131072], P(('events', 'shells')), may hold values from -6 to 6
- pick_weight: float32 [131072], P(('events', 'shells')), may hold values from 0.2 to 15
- station: int32 [131072], P(('events', 'shells')), may hold values from 0 to 2047
Outputs:
- gradient: float32 [1048576], P('shells')
- correction: float32 [2048], replicated
- weighted: float32 [131072], P(('events', 'shells'))
Inputs may be any that keep to these rules, and one draw needn't show every extreme that they name: `blk_count`: each device uses its first slots; some device uses all 512 in every draw. The owner of a slot is pick_block // 64. Among the used slots of one device, at most 64 have one owner; in every event group some owner gets exactly 64 from every device of the group.
All inputs are finite; a program needn't handle non-finite values.
Results may differ from a plain program's by a relative error of at most 0.0026.
Values may be sent and summed in bfloat16 or wider, within the bound.
A program may use at most 64 MiB of HBM per device.

v0:
```python
import jax
import jax.numpy as jnp
from jax import lax
from jax.sharding import PartitionSpec as P

PICK_BLK = 64
CELL_BLK = 128
STATIONS = 2048


def local(model, sensitivity, pick_block, cell_block, blk_count, observed, pick_weight, station):
    slot_count = blk_count[0]
    slot_total = sensitivity.shape[0]
    slot_step = min(32, slot_total)
    model_rows = model.reshape(-1, CELL_BLK)
    owned_picks = observed.shape[0]
    owned_blocks = owned_picks // PICK_BLK
    shell_count = lax.axis_size("shells")
    group_rows = owned_blocks * shell_count
    turns = (slot_count + slot_step - 1) // slot_step

    def slot_range(turn):
        offset = turn * slot_step
        blocks = lax.dynamic_slice_in_dim(sensitivity, offset, slot_step, 0)
        picks_of = lax.dynamic_slice_in_dim(pick_block, offset, slot_step, 0)
        cells_of = lax.dynamic_slice_in_dim(cell_block, offset, slot_step, 0)
        alive = offset + jnp.arange(slot_step, dtype=jnp.int32) < slot_count
        return (blocks, picks_of, cells_of, alive)

    def slot_values(turn):
        blocks, picks_of, cells_of, alive = slot_range(turn)
        values = jnp.einsum(
            "kpc,kc->kp", blocks, model_rows[cells_of], preferred_element_type=jnp.float32
        )
        return (jnp.where(alive[:, None], values, 0.0), picks_of)

    def forward_turn(turn, partials):
        values, picks_of = slot_values(turn)
        return partials.at[picks_of].add(values)

    partials = lax.fori_loop(0, turns, forward_turn, jnp.zeros((group_rows, PICK_BLK), jnp.float32))
    flat_terms = partials.reshape(-1)
    summed = lax.psum(flat_terms, "shells")
    predicted = lax.dynamic_slice_in_dim(
        summed, lax.axis_index("shells") * owned_picks, owned_picks, 0
    )
    misfit = observed - predicted
    numer_local = jax.ops.segment_sum(pick_weight * misfit, station, num_segments=STATIONS)
    denom_local = jax.ops.segment_sum(pick_weight, station, num_segments=STATIONS)
    numer, denom = lax.psum((numer_local, denom_local), ("events", "shells"))
    correction = numer / (denom + 1.0)
    weighted = pick_weight * (misfit - correction[station])
    weighted_half = weighted.astype(jnp.bfloat16)
    group_resid = lax.all_gather(weighted_half, "shells", axis=0, tiled=True).reshape(
        group_rows, PICK_BLK
    )

    def backward_turn(turn, grads):
        blocks, picks_of, cells_of, alive = slot_range(turn)
        terms = jnp.einsum(
            "kpc,kp->kc", blocks, group_resid[picks_of], preferred_element_type=jnp.float32
        )
        terms = jnp.where(alive[:, None], terms, 0.0)
        return grads.at[cells_of].add(terms)

    grads = lax.fori_loop(0, turns, backward_turn, jnp.zeros(model_rows.shape, jnp.float32))
    gradient = lax.psum(grads.reshape(-1), "events")
    return (gradient, correction, weighted)


def solution(mesh):
    placed = (
        P("shells"),
        P(("events", "shells"), None, None),
        P(("events", "shells")),
        P(("events", "shells")),
        P(("events", "shells")),
        P(("events", "shells")),
        P(("events", "shells")),
        P(("events", "shells")),
    )
    return jax.shard_map(
        local,
        mesh=mesh,
        in_specs=placed,
        out_specs=(P("shells"), P(), P(("events", "shells"))),
        check_vma=False,
    )
```

profile of v0, /device:TPU:0, one launch (start us, length us, event | category | flops | bytes accessed | tf_op | source)
XLA Modules:
  0.0 394.1 jit_solution(14609551671083954351)
XLA Ops:
  7.9 27.2 %while.20 = (s32[]{:T(128)}, f32[1024,64]{1,0:T(8,128)S(1)}, s32[]{:T(128)}, s32[512]{0:T(512)}, s32[]{:T(128)}, /*index=5*/bf16[512,64,128]{2,1,0:T(8,128)(2,1)...) while((s32[]{:T(128)}, f32[1024,64]{1,0:T(8,128)S(1)}, ...), condition=%wide.region_2.3_spmd, body=%wide.region_0.2_spmd.sunk | while | flops 529670 | bytes 841183 | solution.py:41
  7.9 0.8 compare_select_fusion.7
  8.7 1.5 gather_fusion
  10.2 1.4 fusion.34
  12.3 1.0 scatter_custom_fusion.13
  13.4 0.8 compare_select_fusion.7
  14.2 1.5 gather_fusion
  15.7 1.4 fusion.34
  17.8 1.0 scatter_custom_fusion.13
  18.8 0.8 compare_select_fusion.7
  19.6 1.5 gather_fusion
  21.1 1.4 fusion.34
  23.2 1.0 scatter_custom_fusion.13
  24.2 0.8 compare_select_fusion.7
  25.0 1.5 gather_fusion
  26.5 1.4 fusion.34
  28.6 1.0 scatter_custom_fusion.13
  29.7 0.8 compare_select_fusion.7
  30.5 1.5 gather_fusion
  32.0 1.4 fusion.34
  34.1 1.0 scatter_custom_fusion.13
  35.1 0.8 reshape.29
  36.0 22.1 %scatter_custom_fusion.3 = f32[2048]{0:T(1024)S(1)} fusion(s32[4096]{0:T(1024)} %param.19, f32[4096]{0:T(1024)} %param.18, f32[]{:T(128)} %constant.36.clone.1), kind=kCustom, calls=%fused_computation.37 | custom fusion | flops 4096 | bytes 8704 | tf_op jit(solution)/shard_map/scatter-add | solution.py:49
  58.9 127.5 %all-reduce.4.cloned.1.call-done = f32[65536]{0:T(1024)} async-done(((f32[65536]{0:T(1024)}), f32[65536]{0:T(1024)}) %all-reduce.4.cloned.1.call-update) | async-done | bytes 262160 | tf_op jit(solution)/shard_map/psum | solution.py:43
  186.4 0.8 fusion.17
  187.1 22.1 %scatter_custom_fusion.2 = f32[2048]{0:T(1024)S(1)} fusion(s32[4096]{0:T(1024)} %param.19, f32[4096]{0:T(1024)S(1)} %fusion.17, f32[]{:T(128)} %constant.36.clone.1), kind=kCustom, calls=%fused_computation.39 | custom fusion | flops 4096 | bytes 8704 | tf_op jit(solution)/shard_map/scatter-add | solution.py:48
  209.3 41.0 %all-reduce = (f32[2048]{0:T(1024)S(1)}, f32[2048]{0:T(1024)S(1)}) all-reduce(f32[2048]{0:T(1024)S(1)} %scatter_custom_fusion.2, f32[2048]{0:T(1024)S(1)} %scatter_custom_fusion.3), channel_id=1, replica_groups=mesh['events'=2,'shells'=16] {'events','shells'}, use_global_device_ids=true, to_apply=%region_5.6 | all-reduce | flops 4096 | bytes 32768 | tf_op jit(solution)/shard_map/psum | solution.py:50
  250.3 23.0 %gather_fusion.2 = f32[4096]{0:T(1024)S(1)} fusion(f32[2048]{0:T(1024)S(1)} %add_divide_fusion, s32[4096]{0:T(1024)S(1)} %fusion.16), kind=kCustom, calls=%fused_computation.2 | custom fusion | bytes 49152 | tf_op jit(solution)/shard_map/gather | solution.py:52
  273.3 1.3 fusion.22
  274.7 21.5 %all_gather.3 = bf16[65536]{0:T(1024)(128)(2,1)S(1)} all-gather(bf16[4096]{0:T(1024)(128)(2,1)S(1)} %get-tuple-element.125), channel_id=1, replica_groups=mesh['events'=2,'shells'=16] {'shells'}, dimensions={0}, use_global_device_ids=true | all-gather | bytes 139264 | tf_op jit(solution)/shard_map/all_gather | solution.py:54
  296.3 21.5 %while.21 = (s32[]{:T(128)}, f32[512,128]{1,0:T(8,128)S(1)}, s32[]{:T(128)}, s32[512]{0:T(512)}, s32[]{:T(128)}, /*index=5*/bf16[512,64,128]{2,1,0:T(8,128)(2,1)...) while((s32[]{:T(128)}, f32[512,128]{1,0:T(8,128)S(1)}, ...), condition=%wide.region_10.11_spmd, body=%wide.region_8.10_spmd.sunk | while | flops 533766 | bytes 837087 | solution.py:66
  296.3 0.8 compare_select_fusion.8
  297.7 1.3 fusion.38
  299.7 0.9 scatter_custom_fusion.15
  300.6 0.8 compare_select_fusion.8
  302.0 1.3 fusion.38
  304.0 0.9 scatter_custom_fusion.15
  304.9 0.8 compare_select_fusion.8
  306.3 1.3 fusion.38
  308.3 0.9 scatter_custom_fusion.15
  309.2 0.8 compare_select_fusion.8
  310.6 1.3 fusion.38
  312.5 0.9 scatter_custom_fusion.15
  313.5 0.8 compare_select_fusion.8
  314.9 1.3 fusion.38
  316.8 0.9 scatter_custom_fusion.15
  318.5 67.1 %all-reduce.6.cloned.1.call-done = f32[65536]{0:T(1024)} async-done(((f32[65536]{0:T(1024)}), f32[65536]{0:T(1024)}) %all-reduce.6.cloned.1.call-update) | async-done | bytes 262160 | tf_op jit(solution)/shard_map/psum | solution.py:67
  385.6 1.7 copy.40
  (42 shorter events, 11.5 us)
Async XLA Ops:
  7.2 179.2 %all-reduce.4.cloned.1.call-start = ((), (), s32[]{:S(2)}) async-start(), calls=%async_computation | async-start | bytes 524288 | tf_op jit(solution)/shard_map/psum | solution.py:43
  36.0 349.6 %all-reduce.6.cloned.1.call-start = ((), (), s32[]{:S(2)}) async-start(), calls=%async_computation.1 | async-start | bytes 524288 | tf_op jit(solution)/shard_map/psum | solution.py:67
  250.2 23.1 %copy-start = (f32[2048]{0:T(1024)}, f32[2048]{0:T(1024)S(1)}, u32[]{:S(2)}) copy-start(f32[2048]{0:T(1024)S(1)} %add_divide_fusion) | copy-start | bytes 24580
  250.2 23.1 %copy-start.2 = (f32[4096]{0:T(1024)S(1)}, f32[4096]{0:T(1024)}, u32[]{:S(2)}) copy-start(f32[4096]{0:T(1024)} %param.18) | copy-start | bytes 49156
  250.3 23.1 %copy-start.3 = (f32[4096]{0:T(1024)S(1)}, f32[4096]{0:T(1024)}, u32[]{:S(2)}) copy-start(f32[4096]{0:T(1024)} %param.17) | copy-start | bytes 49156
  317.8 0.7 copy-start.1
Sparse Core Ops, SparseCore 0:
  36.1 150.2 all-reduce.3
  318.6 66.8 all-reduce.5
where the time goes:
time: 396 us; the launch traced here: 394 us
  waiting for transfers between devices  195 us (49%)
  other arithmetic  71.4 us (18%)
  blocking collectives  62.4 us (16%)
  local copies, waits for them, and re-layouts  36.9 us (9%)
  between operations  14.8 us (4%)
  matrix products  13.4 us (3%)
    psum x1, waiting for transfers between devices, local(): summed = lax.psum(flat_terms, 'shells')  128 us
    psum x1, waiting for transfers between devices, local(): gradient = lax.psum(grads.reshape(-1), 'events')  67.1 us
    psum x1, blocking collectives, local(): numer, denom = lax.psum((numer_local, denom_local), ('events', 'shells'))  41 us
    gather x1, local copies, waits for them, and re-layouts, local(): weighted = pick_weight * (misfit - correction[station])  23 us
    scatter-add x1, other arithmetic, local(): jax.ops.segment_sum(pick_weight * misfit, station, num_segments=STATIONS)  22.1 us
    scatter-add x1, other arithmetic, local(): jax.ops.segment_sum(pick_weight, station, num_segments=STATIONS)  22.1 us
    all_gather x1, blocking collectives, local(): lax.all_gather(weighted_half, 'shells', axis=0, tiled=True)  21.5 us
  transfers between devices with their start and end apart: 2, of which 2 were waited for; matrix products, arithmetic and copies ran while one was open for 6% of the time, Pallas kernels for 0%

commit v1 on v0

v1 whole, which is shorter than its diff:
```python
import functools

import jax
import jax.numpy as jnp
from jax import lax
from jax.experimental import pallas as pl
from jax.experimental.pallas import tpu as pltpu
from jax.sharding import PartitionSpec as P

PICK_BLK = 64
CELL_BLK = 128
STATIONS = 2048
LANES = 128
GROUP = 16
STEPS = 8
MESH = pl.DeviceIdType.MESH
F32 = jnp.float32
BF16 = jnp.bfloat16


def dot_nn(a, b):
    return lax.dot_general(a, b, (((1,), (0,)), ((), ())), preferred_element_type=F32)


def dot_nt(a, b):
    return lax.dot_general(a, b, (((1,), (1,)), ((), ())), preferred_element_type=F32)


def dot_tn(a, b):
    return lax.dot_general(a, b, (((0,), (0,)), ((), ())), preferred_element_type=F32)


def parts_of(x, count):
    parts = []
    for _ in range(count):
        part = x.astype(BF16)
        parts.append(part)
        x = x - part.astype(F32)
    return parts


def one_hot(rows, index_row, keep=None):
    shape = (rows, index_row.shape[1])
    hit = lax.broadcasted_iota(jnp.int32, shape, 0) == index_row
    if keep is not None:
        hit = jnp.logical_and(hit, keep)
    return jnp.where(hit, 1.0, 0.0).astype(BF16)


def diagonal_mask(j):
    row = lax.broadcasted_iota(jnp.int32, (GROUP, LANES), 0)
    lane = lax.broadcasted_iota(jnp.int32, (GROUP, LANES), 1)
    return row == 2 * j + lane // PICK_BLK


def swap_halves(x):
    return pltpu.roll(x, PICK_BLK, 1)


def halves(rows):
    return lax.broadcasted_iota(jnp.int32, (rows, LANES), 1) < PICK_BLK


def forward_kernel(count_ref, blocks_ref, model_ref, pick_ref, cell_ref, out_ref, gathered, values):
    step = pl.program_id(0)
    slots = values.shape[0]
    per_step = slots // STEPS

    @pl.when(step == 0)
    def _():
        hot = one_hot(model_ref.shape[0], cell_ref[...])
        gathered[...] = dot_tn(hot, model_ref[...]).astype(BF16)

    for g in range(per_step // GROUP):
        first = pl.multiple_of(step * per_step + g * GROUP, GROUP)
        rows = gathered[pl.ds(first, GROUP), :]
        block = blocks_ref[g * GROUP * PICK_BLK:(g + 1) * GROUP * PICK_BLK, :]
        full = dot_nt(rows, block)
        total = jnp.zeros((GROUP, LANES), F32)
        for j in range(GROUP // 2):
            total = total + jnp.where(diagonal_mask(j), full[:, j * LANES:(j + 1) * LANES], 0.0)
        values[pl.ds(first, GROUP), :] = total

    @pl.when(step == STEPS - 1)
    def _():
        v = values[...]
        v = v + swap_halves(v)
        terms = jnp.concatenate(parts_of(v, 2), axis=1)
        pick = pick_ref[...]
        alive = lax.broadcasted_iota(jnp.int32, (1, slots), 1) < count_ref[0]
        rows = out_ref.shape[0]
        low = dot_nn(one_hot(rows, pick // 2, jnp.logical_and(alive, pick % 2 == 0)), terms)
        high = dot_nn(one_hot(rows, pick // 2, jnp.logical_and(alive, pick % 2 == 1)), terms)
        both = jnp.where(
            lax.broadcasted_iota(jnp.int32, (rows, 2 * LANES), 1) % LANES < PICK_BLK, low, high
        )
        out_ref[...] = both[:, :LANES] + both[:, LANES:]


def backward_kernel(count_ref, blocks_ref, resid_ref, pick_ref, cell_ref, out_ref, gathered, terms):
    step = pl.program_id(0)
    slots = terms.shape[0]
    per_step = slots // STEPS

    @pl.when(step == 0)
    def _():
        pick = pick_ref[...]
        rows = resid_ref.shape[0]
        low = dot_tn(one_hot(rows, pick // 2, pick % 2 == 0), resid_ref[...])
        high = dot_tn(one_hot(rows, pick // 2, pick % 2 == 1), resid_ref[...])
        picked = jnp.where(halves(slots), low, high)
        gathered[...] = picked + swap_halves(picked)

    for g in range(per_step // GROUP):
        first = pl.multiple_of(step * per_step + g * GROUP, GROUP)
        rows = gathered[pl.ds(first, GROUP), :]
        spread = jnp.concatenate(
            [jnp.where(diagonal_mask(j), rows, 0.0).astype(BF16) for j in range(GROUP // 2)], axis=1
        )
        block = blocks_ref[g * GROUP * PICK_BLK:(g + 1) * GROUP * PICK_BLK, :]
        terms[pl.ds(first, GROUP), :] = dot_nn(spread, block)

    @pl.when(step == STEPS - 1)
    def _():
        alive = lax.broadcasted_iota(jnp.int32, (1, slots), 1) < count_ref[0]
        hot = one_hot(out_ref.shape[0], cell_ref[...], alive)
        both = dot_nn(hot, jnp.concatenate(parts_of(terms[...], 2), axis=1))
        out_ref[...] = both[:, :LANES] + both[:, LANES:]


def middle_kernel(
    n_events, n_shells,
    partial_ref, observed_ref, weight_ref, station_ref,
    resid_ref, correction_ref, weighted_ref,
    landed, low_hot, spread, sums_out, sums_in, fitted,
    send_a, recv_a, send_b, recv_b, send_c, recv_c, send_d, recv_d,
):
    event = lax.axis_index("events")
    shell = lax.axis_index("shells")
    n_devices = n_events * n_shells
    mine = event * n_shells + shell
    rows = observed_ref.shape[0]
    n_high = sums_out.shape[0]

    barrier = pltpu.get_barrier_semaphore()

    def greet(i, carry):
        other = lax.rem(mine + i, n_devices)
        pl.semaphore_signal(
            barrier, inc=1, device_id=(other // n_shells, lax.rem(other, n_shells)),
            device_id_type=MESH,
        )
        return carry

    lax.fori_loop(1, n_devices, greet, 0)
    pl.semaphore_wait(barrier, n_devices - 1)

    def shell_at(i):
        return lax.rem(shell + i, n_shells)

    def shell_from(i):
        return lax.rem(shell + n_shells - i, n_shells)

    def partial_copy(i, source):
        other = shell_at(i)
        return pltpu.make_async_remote_copy(
            src_ref=partial_ref.at[pl.ds(pl.multiple_of(other * rows, rows), rows), :],
            dst_ref=landed.at[source],
            send_sem=send_a.at[i],
            recv_sem=recv_a.at[source],
            device_id=(event, other),
            device_id_type=MESH,
        )

    def start_partial(i, carry):
        partial_copy(i, shell).start()
        return carry

    lax.fori_loop(1, n_shells, start_partial, 0)

    station = station_ref[...]
    high, low = station // LANES, lax.rem(station, LANES)
    for r in range(rows):
        low_hot[:, r * LANES:(r + 1) * LANES] = one_hot(LANES, low[r:r + 1, :])
    high_id = lax.broadcasted_iota(jnp.int32, (n_high, LANES), 0)

    def station_sums(x):
        pieces = parts_of(x, 3)
        for r in range(rows):
            hit = high_id == high[r:r + 1, :]
            for k in range(3):
                piece = pieces[k][r:r + 1, :].astype(F32)
                spread[k * n_high:(k + 1) * n_high, r * LANES:(r + 1) * LANES] = jnp.where(
                    hit, piece, 0.0
                ).astype(BF16)
        out = dot_nt(spread[...], low_hot[...])
        return out[:n_high] + (out[n_high:2 * n_high] + out[2 * n_high:])

    weight = weight_ref[...]
    denom = station_sums(weight)
    for h in range(n_high):
        sums_out[h, 1:2, :] = denom[h:h + 1, :]

    def take_partial(i, total):
        source = shell_from(i)
        partial_copy(i, source).wait_recv()
        return total + landed[source]

    own = partial_ref[pl.ds(pl.multiple_of(shell * rows, rows), rows), :]
    predicted = lax.fori_loop(1, n_shells, take_partial, own)
    misfit = observed_ref[...] - predicted
    numer = station_sums(weight * misfit)
    for h in range(n_high):
        sums_out[h, 0:1, :] = numer[h:h + 1, :]

    def sums_copy(i, source):
        other = lax.rem(mine + i, n_devices)
        other_shell = lax.rem(other, n_shells)
        return pltpu.make_async_remote_copy(
            src_ref=sums_out.at[other_shell],
            dst_ref=sums_in.at[source],
            send_sem=send_b.at[i],
            recv_sem=recv_b.at[source],
            device_id=(other // n_shells, other_shell),
            device_id_type=MESH,
        )

    def start_sums(i, carry):
        sums_copy(i, mine).start()
        return carry

    lax.fori_loop(1, n_devices, start_sums, 0)
    sums_in[mine] = sums_out[shell]

    def wait_sums(i, carry):
        sums_copy(i, lax.rem(mine + n_devices - i, n_devices)).wait_recv()
        return carry

    lax.fori_loop(1, n_devices, wait_sums, 0)

    def add_sums(d, total):
        return total + sums_in[d]

    total = lax.fori_loop(1, n_devices, add_sums, sums_in[0])
    fitted[shell] = total[0:1, :] / (total[1:2, :] + 1.0)

    def fitted_copy(i, source):
        return pltpu.make_async_remote_copy(
            src_ref=fitted.at[source],
            dst_ref=fitted.at[source],
            send_sem=send_c.at[i],
            recv_sem=recv_c.at[source],
            device_id=(event, shell_at(i)),
            device_id_type=MESH,
        )

    def start_fitted(i, carry):
        fitted_copy(i, shell).start()
        return carry

    def wait_fitted(i, carry):
        fitted_copy(i, shell_from(i)).wait_recv()
        return carry

    lax.fori_loop(1, n_shells, start_fitted, 0)
    lax.fori_loop(1, n_shells, wait_fitted, 0)

    correction = jnp.concatenate([fitted[h] for h in range(n_high)], axis=0)
    correction_ref[...] = correction[:correction_ref.shape[0]]
    pieces = jnp.concatenate(parts_of(correction, 3), axis=0)
    wide = dot_nn(pieces, low_hot[...])
    wide = wide[:n_high] + (wide[n_high:2 * n_high] + wide[2 * n_high:])
    picked = []
    for r in range(rows):
        hit = high_id == high[r:r + 1, :]
        picked.append(
            jnp.sum(jnp.where(hit, wide[:, r * LANES:(r + 1) * LANES], 0.0), axis=0, keepdims=True)
        )
    weighted = weight * (misfit - jnp.concatenate(picked, axis=0))
    weighted_ref[...] = weighted
    resid_ref[shell] = weighted.astype(BF16)

    def resid_copy(i, source):
        return pltpu.make_async_remote_copy(
            src_ref=resid_ref.at[source],
            dst_ref=resid_ref.at[source],
            send_sem=send_d.at[i],
            recv_sem=recv_d.at[source],
            device_id=(event, shell_at(i)),
            device_id_type=MESH,
        )

    def start_resid(i, carry):
        resid_copy(i, shell).start()
        return carry

    def wait_resid(i, carry):
        resid_copy(i, shell_from(i)).wait_recv()
        return carry

    lax.fori_loop(1, n_shells, start_resid, 0)
    lax.fori_loop(1, n_shells, wait_resid, 0)

    def sent(i, carry):
        partial_copy(i, shell).wait_send()
        fitted_copy(i, shell).wait_send()
        resid_copy(i, shell).wait_send()
        return carry

    def sums_sent(i, carry):
        sums_copy(i, mine).wait_send()
        return carry

    lax.fori_loop(1, n_shells, sent, 0)
    lax.fori_loop(1, n_devices, sums_sent, 0)


def local(n_events, n_shells, model, sensitivity, pick_block, cell_block, blk_count, observed, pick_weight, station):
    slots = sensitivity.shape[0]
    cells = model.shape[0] // CELL_BLK
    rows = observed.shape[0] // LANES
    group_rows = rows * n_shells
    high_rows = STATIONS // LANES
    n_high = max(high_rows, n_shells)
    blocks = sensitivity.reshape(slots * PICK_BLK, CELL_BLK)
    pick = pick_block.reshape(1, slots)
    cell = cell_block.reshape(1, slots)
    chunk = slots // STEPS * PICK_BLK
    whole = lambda *shape: pl.BlockSpec(shape, lambda i: (0,) * len(shape))
    params = pltpu.CompilerParams(
        dimension_semantics=("arbitrary",), vmem_limit_bytes=48 * 1024 * 1024
    )
    cost = pl.CostEstimate(
        flops=2 * slots * PICK_BLK * CELL_BLK,
        bytes_accessed=2 * slots * PICK_BLK * CELL_BLK,
        transcendentals=0,
    )
    count_spec = pl.BlockSpec(memory_space=pltpu.SMEM)
    blocks_spec = pl.BlockSpec((chunk, CELL_BLK), lambda i: (i, 0))

    partial = pl.pallas_call(
        forward_kernel,
        grid=(STEPS,),
        out_shape=jax.ShapeDtypeStruct((group_rows, LANES), F32),
        in_specs=[
            count_spec, blocks_spec, whole(cells, CELL_BLK), whole(1, slots), whole(1, slots),
        ],
        out_specs=whole(group_rows, LANES),
        scratch_shapes=[pltpu.VMEM((slots, CELL_BLK), BF16), pltpu.VMEM((slots, LANES), F32)],
        compiler_params=params,
        cost_estimate=cost,
    )(blk_count, blocks, model.reshape(cells, CELL_BLK), pick, cell)

    n_devices = n_events * n_shells
    dma = lambda n: pltpu.SemaphoreType.DMA((n,))
    resid, correction, weighted = pl.pallas_call(
        functools.partial(middle_kernel, n_events, n_shells),
        out_shape=(
            jax.ShapeDtypeStruct((n_shells, rows, LANES), BF16),
            jax.ShapeDtypeStruct((high_rows, LANES), F32),
            jax.ShapeDtypeStruct((rows, LANES), F32),
        ),
        in_specs=[pl.BlockSpec(memory_space=pltpu.VMEM)] * 4,
        out_specs=(pl.BlockSpec(memory_space=pltpu.VMEM),) * 3,
        scratch_shapes=[
            pltpu.VMEM((n_shells, rows, LANES), F32),
            pltpu.VMEM((LANES, rows * LANES), BF16),
            pltpu.VMEM((3 * n_high, rows * LANES), BF16),
            pltpu.VMEM((n_high, 2, LANES), F32),
            pltpu.VMEM((n_devices, 2, LANES), F32),
            pltpu.VMEM((n_high, 1, LANES), F32),
            dma(n_shells), dma(n_shells), dma(n_devices), dma(n_devices),
            dma(n_shells), dma(n_shells), dma(n_shells), dma(n_shells),
        ],
        compiler_params=pltpu.CompilerParams(
            collective_id=0, has_side_effects=True, vmem_limit_bytes=48 * 1024 * 1024
        ),
    )(
        partial,
        observed.reshape(rows, LANES),
        pick_weight.reshape(rows, LANES),
        station.reshape(rows, LANES),
    )

    grads = pl.pallas_call(
        backward_kernel,
        grid=(STEPS,),
        out_shape=jax.ShapeDtypeStruct((cells, CELL_BLK), F32),
        in_specs=[
            count_spec, blocks_spec, whole(group_rows, LANES), whole(1, slots), whole(1, slots),
        ],
        out_specs=whole(cells, CELL_BLK),
        scratch_shapes=[pltpu.VMEM((slots, LANES), F32), pltpu.VMEM((slots, CELL_BLK), F32)],
        compiler_params=params,
        cost_estimate=cost,
    )(blk_count, blocks, resid.reshape(group_rows, LANES), pick, cell)

    if n_events == 2:
        other = lax.ppermute(grads, "events", [(0, 1), (1, 0)])
        gradient = grads + other
    else:
        gradient = lax.psum(grads, "events")
    return (gradient.reshape(-1), correction.reshape(-1), weighted.reshape(-1))


def solution(mesh):
    every = P(("events", "shells"))
    placed = (P("shells"), P(("events", "shells"), None, None)) + (every,) * 6
    return jax.shard_map(
        functools.partial(local, mesh.shape["events"], mesh.shape["shells"]),
        mesh=mesh,
        in_specs=placed,
        out_specs=(P("shells"), P(), every),
        check_vma=False,
    )
```

time: 396 us -> 60.4 us (0.15)
  waiting for transfers between devices: 195 us -> 7.2 us
  other arithmetic: 71.4 us -> 0.73 us
  blocking collectives: 62.4 us -> 0 us
  Pallas kernels: 0 us -> 46 us
  local copies, waits for them, and re-layouts: 36.9 us -> 3.48 us
  between operations: 14.8 us -> 1.39 us
  matrix products: 13.4 us -> 0 us
    psum x2 -> x0, waiting for transfers between devices: 195 us -> none  [the longest x1 128 us: local(): summed = lax.psum(flat_terms, 'shells')]
    scatter-add x12 -> x0, other arithmetic: 54 us -> none  [the longest x1 22.1 us: local(): jax.ops.segment_sum(pick_weight * misfit, station, num_segments=STATIONS)]
    pallas_call x0 -> x3, Pallas kernels: none -> 46 us  [the longest x1 30.6 us: local(): pl.pallas_call(functools.partial(middle_kernel, n_events, n_shells), out_...]
    psum x1 -> x0, blocking collectives: 41 us -> none  [local(): numer, denom = lax.psum((numer_local, denom_local), ('events', 'shells'))]
    gather x11 -> x0, local copies, waits for them, and re-layouts: 33.5 us -> none  [the longest x1 23 us: local(): weighted = pick_weight * (misfit - correction[station])]
    all_gather x1 -> x0, blocking collectives: 21.5 us -> none  [local(): lax.all_gather(weighted_half, 'shells', axis=0, tiled=True)]
    dot_general x10 -> x0, matrix products: 13.4 us -> none  [the longest x5 7.01 us: slot_values(): jnp.einsum('kpc,kc->kp', blocks, model_rows[cells_of], preferred_element_...]
    select_n x10 -> x0, other arithmetic: 7.81 us -> none  [the longest x5 3.9 us: backward_turn(): group_resid[picks_of]]
  transfers between devices with their start and end apart: 2 -> 1, of which waited for: 2 -> 1; matrix products, arithmetic and copies ran while one was open for 6% -> 0% of each run, Pallas kernels for 0% -> 0%
where the time goes in v1:
time: 60.4 us; the launch traced here: 59.9 us
  Pallas kernels  46 us (76%)
  waiting for transfers between devices  7.2 us (12%)
  local copies, waits for them, and re-layouts  3.48 us (6%)
  between operations  1.39 us (2%)
  starting transfers between devices  1.18 us (2%)
  other arithmetic  0.73 us (1%)
    pallas_call x1, Pallas kernels, local(): pl.pallas_call(functools.partial(middle_kernel, n_events, n_shells), out_...  30.6 us
    pallas_call x1, Pallas kernels, local(): pl.pallas_call(forward_kernel, grid=(STEPS,), out_shape=jax.ShapeDtypeStr...  8.01 us
    pallas_call x1, Pallas kernels, local(): pl.pallas_call(backward_kernel, grid=(STEPS,), out_shape=jax.ShapeDtypeSt...  7.35 us
    ppermute x1, waiting for transfers between devices, local(): other = lax.ppermute(grads, 'events', [(0, 1), (1, 0)])  7.2 us
    unnamed x18, local copies, waits for them, and re-layouts  3.48 us
  transfers between devices with their start and end apart: 1, of which 1 were waited for; matrix products, arithmetic and copies ran while one was open for 0% of the time, Pallas kernels for 0%

profile of v1, /device:TPU:0, one launch (start us, length us, event | category | flops | bytes accessed | tf_op | source)
XLA Modules:
  0.0 59.9 jit_solution(14016091779344376250)
XLA Ops:
  0.6 0.0 copy-start.7
  0.6 0.0 copy-start.5
  1.3 0.0 copy-start
  1.3 0.9 %copy-done = bf16[65536]{0:T(1024)(128)(2,1)S(1)} copy-done((bf16[65536]{0:T(1024)(128)(2,1)S(1)}, bf16[65536]{0:T(1024)(128)(2,1)}, u32[]{:S(2)}) %copy-start) | copy-done | bytes 131096
  2.2 0.0 copy-start.4
  2.2 0.7 %copy-done.4 = s32[512]{0:T(512)S(1)} copy-done((s32[512]{0:T(512)S(1)}, s32[512]{0:T(512)}, u32[]{:S(2)}) %copy-start.4) | copy-done | bytes 2072
  2.9 0.0 copy-start.6
  2.9 0.7 %copy-done.6 = s32[512]{0:T(512)S(1)} copy-done((s32[512]{0:T(512)S(1)}, s32[512]{0:T(512)}, u32[]{:S(2)}) %copy-start.6) | copy-done | bytes 2072
  3.6 0.0 copy-start.1
  3.6 0.0 copy-start.2
  3.6 0.0 copy-start.3
  3.6 8.0 %shard_map.103.partial_ref = f32[512,128]{1,0:T(8,128)S(1)} custom-call(s32[1]{0:T(128)S(6)} %copy.13.count_ref, bf16[32768,128]{1,0:T(8,128)(2,1)} %bitcast.23, bf16[512,128]{1,0:T(8,128)(2,1)S(1)} %bitcast.12, s32[1,512]{1,0:T(1,128)S(1)} %bitcast.19, s32[1,512]{1,0:T(1,128)S(1)} %bitcast.21), custom_call_target="tpu_custom_call" | custom-call | flops 8388608 | bytes 8388608 | tf_op jit(solution)/shard_map/pallas_call | solution.py:341
  11.6 0.0 copy-done.1
  11.6 0.0 copy-done.2
  11.6 0.0 copy-done.3
  11.6 30.6 %shard_map.104 = (bf16[16,32,128]{2,1,0:T(8,128)(2,1)S(1)}, f32[16,128]{1,0:T(8,128)S(1)}, f32[32,128]{1,0:T(8,128)S(1)}) custom-call(f32[512,128]{1,0:T(8,128)S(1)} %shard_map.103.partial_ref, f32[32,128]{1,0:T(8,128)S(1)} %bitcast.14, f32[32,128]{1,0:T(8,128)S(1)} %bitcast.15, s32[32,128]{1,0:T(8,128)S(1)} %bitcast.16), custom_call_target="tpu_custom_call" | custom-call | tf_op jit(solution)/shard_map/pallas_call | solution.py:356
  42.2 0.0 copy-done.7
  42.2 0.0 copy-done.5
  42.3 7.4 %shard_map.105 = f32[512,128]{1,0:T(8,128)S(1)} custom-call(s32[1]{0:T(128)S(6)} %copy.13.count_ref, bf16[32768,128]{1,0:T(8,128)(2,1)} %bitcast.24, bf16[512,128]{1,0:T(8,128)(2,1)S(1)} %bitcast.13, s32[1,512]{1,0:T(1,128)S(1)} %bitcast.20, s32[1,512]{1,0:T(1,128)S(1)} %bitcast.22), custom_call_target="tpu_custom_call" | custom-call | flops 8388608 | bytes 8388608 | tf_op jit(solution)/shard_map/pallas_call | solution.py:385
  49.6 1.2 %collective-permute-start = (f32[512,128]{1,0:T(8,128)S(1)}, f32[512,128]{1,0:T(8,128)S(1)}, u32[]{:S(2)}, u32[]{:S(2)}) collective-permute-start(f32[512,128]{1,0:T(8,128)S(1)} %shard_map.105), channel_id=1, source_target_pairs={{0,16},{16,0},{1,17},{17,1},{2,18},{18,2},{3,19},{19,3},{4,20},{20... | collective-permute-start | bytes 786440 | tf_op jit(solution)/shard_map/ppermute | solution.py:399
  50.8 7.2 %collective-permute-done = f32[512,128]{1,0:T(8,128)S(1)} collective-permute-done((f32[512,128]{1,0:T(8,128)S(1)}, f32[512,128]{1,0:T(8,128)S(1)}, u32[]{:S(2)}, u32[]{:S(2)}) %collective-permute-start) | collective-permute-done | bytes 262176 | tf_op jit(solution)/shard_map/ppermute | solution.py:399
  58.0 0.7 %add_bitcast_fusion = f32[65536]{0:T(1024)} fusion(f32[512,128]{1,0:T(8,128)S(1)} %shard_map.105, f32[512,128]{1,0:T(8,128)S(1)} %collective-permute-done), kind=kLoop, calls=%fused_computation | loop fusion | flops 65536 | bytes 786432 | tf_op jit(solution)/shard_map/reshape | solution.py:403
  58.7 0.6 copy.14
  59.3 0.6 %copy.15 = f32[4096]{0:T(1024)} copy(f32[4096]{0:T(1024)S(1)} %bitcast.17) | data formatting | bytes 32768
Async XLA Ops:
  0.6 41.6 %copy-start.7 = (s32[512]{0:T(512)S(1)}, s32[512]{0:T(512)}, u32[]{:S(2)}) copy-start(s32[512]{0:T(512)} %param.11) | copy-start | bytes 6148
  0.6 41.6 %copy-start.5 = (s32[512]{0:T(512)S(1)}, s32[512]{0:T(512)}, u32[]{:S(2)}) copy-start(s32[512]{0:T(512)} %param.10) | copy-start | bytes 6148
  1.3 0.9 %copy-start = (bf16[65536]{0:T(1024)(128)(2,1)S(1)}, bf16[65536]{0:T(1024)(128)(2,1)}, u32[]{:S(2)}) copy-start(bf16[65536]{0:T(1024)(128)(2,1)} %param.8) | copy-start | bytes 393220
  2.2 0.7 %copy-start.4 = (s32[512]{0:T(512)S(1)}, s32[512]{0:T(512)}, u32[]{:S(2)}) copy-start(s32[512]{0:T(512)} %param.10) | copy-start | bytes 6148
  2.9 0.7 %copy-start.6 = (s32[512]{0:T(512)S(1)}, s32[512]{0:T(512)}, u32[]{:S(2)}) copy-start(s32[512]{0:T(512)} %param.11) | copy-start | bytes 6148
  3.6 8.0 %copy-start.1 = (f32[4096]{0:T(1024)S(1)}, f32[4096]{0:T(1024)}, u32[]{:S(2)}) copy-start(f32[4096]{0:T(1024)} %param.13) | copy-start | bytes 49156
  3.6 8.0 %copy-start.2 = (f32[4096]{0:T(1024)S(1)}, f32[4096]{0:T(1024)}, u32[]{:S(2)}) copy-start(f32[4096]{0:T(1024)} %param.14) | copy-start | bytes 49156
  3.6 8.0 %copy-start.3 = (s32[4096]{0:T(1024)S(1)}, s32[4096]{0:T(1024)}, u32[]{:S(2)}) copy-start(s32[4096]{0:T(1024)} %param.15) | copy-start | bytes 49156
  49.6 8.4 %collective-permute-start = (f32[512,128]{1,0:T(8,128)S(1)}, f32[512,128]{1,0:T(8,128)S(1)}, u32[]{:S(2)}, u32[]{:S(2)}) collective-permute-start(f32[512,128]{1,0:T(8,128)S(1)} %shard_map.105), channel_id=1, source_target_pairs={{0,16},{16,0},{1,17},{17,1},{2,18},{18,2},{3,19},{19,3},{4,20},{20... | collective-permute-start | bytes 786440 | tf_op jit(solution)/shard_map/ppermute | solution.py:399

commit v2 on v1

v2 whole, which is shorter than its diff:
```python
import functools

import jax
import jax.numpy as jnp
from jax import lax
from jax.experimental import pallas as pl
from jax.experimental.pallas import tpu as pltpu
from jax.sharding import PartitionSpec as P

PICK_BLK = 64
CELL_BLK = 128
STATIONS = 2048
LANES = 128
GROUP = 16
CHUNKS = 4
MESH = pl.DeviceIdType.MESH
F32 = jnp.float32
BF16 = jnp.bfloat16


def dot_nn(a, b):
    return lax.dot_general(a, b, (((1,), (0,)), ((), ())), preferred_element_type=F32)


def dot_nt(a, b):
    return lax.dot_general(a, b, (((1,), (1,)), ((), ())), preferred_element_type=F32)


def parts_of(x, count):
    parts = []
    for _ in range(count):
        part = x.astype(BF16)
        parts.append(part)
        x = x - part.astype(F32)
    return parts


def one_hot(rows, index_row):
    shape = (rows, index_row.shape[1])
    hit = lax.broadcasted_iota(jnp.int32, shape, 0) == index_row
    return jnp.where(hit, 1.0, 0.0).astype(BF16)


def diagonal_mask(j):
    row = lax.broadcasted_iota(jnp.int32, (GROUP, LANES), 0)
    lane = lax.broadcasted_iota(jnp.int32, (GROUP, LANES), 1)
    return row == 2 * j + lane // PICK_BLK


def swap_halves(x):
    return pltpu.roll(x, PICK_BLK, 1)


def whole_kernel(
    n_events, n_shells,
    count_ref, blocks_ref, model_ref, pick_ref, cell_ref, observed_ref, weight_ref, station_ref,
    gradient_ref, correction_ref, weighted_ref,
    blocks, pick_hot, pick_hot_t, cell_hot, model_rows, slot_rows, values, partial, landed,
    low_hot, spread, sums_out, sums_in, fitted, resid, grads_out, grads_in,
    load_sem, send_a, recv_a, send_b, recv_b, send_c, recv_c, send_d, recv_d, send_e, recv_e,
):
    event = lax.axis_index("events")
    shell = lax.axis_index("shells")
    n_devices = n_events * n_shells
    mine = event * n_shells + shell
    rows = observed_ref.shape[0]
    n_high = sums_out.shape[0]
    slots = values.shape[0]
    cells = model_ref.shape[0]
    group_rows = partial.shape[0]
    per_chunk = slots // CHUNKS
    chunk_rows = per_chunk * PICK_BLK

    def after(x, i, n):
        return jnp.where(x + i >= n, x + i - n, x + i)

    def before(x, i, n):
        return jnp.where(x >= i, x - i, x + n - i)

    def load(c):
        part = pl.ds(pl.multiple_of(c * chunk_rows, chunk_rows), chunk_rows)
        return pltpu.make_async_copy(blocks_ref.at[part, :], blocks.at[part, :], load_sem.at[c])

    for c in range(CHUNKS):
        load(c).start()

    barrier = pltpu.get_barrier_semaphore()

    def greet_shell(i, carry):
        for j in range(n_events):
            pl.semaphore_signal(
                barrier, inc=1,
                device_id=(after(event, j, n_events), after(shell, i, n_shells)),
                device_id_type=MESH,
            )
        return carry

    for j in range(1, n_events):
        pl.semaphore_signal(
            barrier, inc=1, device_id=(after(event, j, n_events), shell), device_id_type=MESH
        )
    lax.fori_loop(1, n_shells, greet_shell, 0)

    alive = lax.broadcasted_iota(jnp.int32, (1, slots), 1) < count_ref[0]
    pick = jnp.where(alive, pick_ref[...], -2)
    cell = jnp.where(alive, cell_ref[...], -2)
    cell_column = jnp.transpose(jnp.broadcast_to(cell, (LANES, slots)))
    lane = lax.broadcasted_iota(jnp.int32, (slots, LANES), 1)
    found = jnp.zeros((slots, CELL_BLK), F32)
    for b in range(cells // LANES):
        hot = jnp.where(lane + b * LANES == cell_column, 1.0, 0.0).astype(BF16)
        found = found + dot_nn(hot, model_ref[b * LANES:(b + 1) * LANES, :])
    model_rows[...] = found.astype(BF16)
    pick_row = lax.shift_right_arithmetic(pick, 1)
    pick_hot[...] = one_hot(group_rows, pick_row)
    cell_hot[...] = one_hot(cells, cell)
    pick_column = jnp.transpose(jnp.broadcast_to(pick, (LANES, slots)))
    half = (pick_column & 1) == lane // PICK_BLK
    pick_column = lax.shift_right_arithmetic(pick_column, 1)
    for b in range(group_rows // LANES):
        pick_hot_t[:, b * LANES:(b + 1) * LANES] = jnp.where(
            lane + b * LANES == pick_column, 1.0, 0.0
        ).astype(BF16)

    def forward_chunk(c, carry):
        load(c).wait()
        for g in range(per_chunk // GROUP):
            first = pl.multiple_of(c * per_chunk + g * GROUP, GROUP)
            block = blocks[pl.ds(pl.multiple_of(first * PICK_BLK, GROUP * PICK_BLK), GROUP * PICK_BLK), :]
            full = dot_nt(model_rows[pl.ds(first, GROUP), :], block)
            total = jnp.zeros((GROUP, LANES), F32)
            for j in range(GROUP // 2):
                total = total + jnp.where(diagonal_mask(j), full[:, j * LANES:(j + 1) * LANES], 0.0)
            values[pl.ds(first, GROUP), :] = total
        return carry

    lax.fori_loop(0, CHUNKS, forward_chunk, 0)
    v = values[...]
    v = jnp.where(half, v + swap_halves(v), 0.0)
    both = dot_nn(pick_hot[...], jnp.concatenate(parts_of(v, 2), axis=1))
    partial[...] = both[:, :LANES] + both[:, LANES:]

    pl.semaphore_wait(barrier, n_devices - 1)

    def partial_copy(i, source):
        other = after(shell, i, n_shells)
        return pltpu.make_async_remote_copy(
            src_ref=partial.at[pl.ds(pl.multiple_of(other * rows, rows), rows), :],
            dst_ref=landed.at[source],
            send_sem=send_a.at[i],
            recv_sem=recv_a.at[source],
            device_id=(event, other),
            device_id_type=MESH,
        )

    def start_partial(i, carry):
        partial_copy(i, shell).start()
        return carry

    lax.fori_loop(1, n_shells, start_partial, 0)

    station = station_ref[...]
    high, low = station // LANES, lax.rem(station, LANES)
    for r in range(rows):
        low_hot[:, r * LANES:(r + 1) * LANES] = one_hot(LANES, low[r:r + 1, :])
    high_id = lax.broadcasted_iota(jnp.int32, (n_high, LANES), 0)

    def station_sums(x):
        pieces = parts_of(x, 3)
        for r in range(rows):
            hit = high_id == high[r:r + 1, :]
            for k in range(3):
                piece = pieces[k][r:r + 1, :].astype(F32)
                spread[k * n_high:(k + 1) * n_high, r * LANES:(r + 1) * LANES] = jnp.where(
                    hit, piece, 0.0
                ).astype(BF16)
        out = dot_nt(spread[...], low_hot[...])
        return out[:n_high] + (out[n_high:2 * n_high] + out[2 * n_high:])

    weight = weight_ref[...]
    denom = station_sums(weight)
    for h in range(n_high):
        sums_out[h, 1:2, :] = denom[h:h + 1, :]

    def take_partial(i, total):
        source = before(shell, i, n_shells)
        partial_copy(i, source).wait_recv()
        return total + landed[source]

    own = partial[pl.ds(pl.multiple_of(shell * rows, rows), rows), :]
    predicted = lax.fori_loop(1, n_shells, take_partial, own)
    misfit = observed_ref[...] - predicted
    numer = station_sums(weight * misfit)
    for h in range(n_high):
        sums_out[h, 0:1, :] = numer[h:h + 1, :]

    def sums_copy(i, j, source):
        other = after(shell, i, n_shells)
        return pltpu.make_async_remote_copy(
            src_ref=sums_out.at[other],
            dst_ref=sums_in.at[source],
            send_sem=send_b.at[i * n_events + j],
            recv_sem=recv_b.at[source],
            device_id=(after(event, j, n_events), other),
            device_id_type=MESH,
        )

    def sums_from(i, j):
        return before(event, j, n_events) * n_shells + before(shell, i, n_shells)

    def start_sums(i, carry):
        for j in range(n_events):
            sums_copy(i, j, mine).start()
        return carry

    def wait_sums(i, carry):
        for j in range(n_events):
            sums_copy(i, j, sums_from(i, j)).wait_recv()
        return carry

    for j in range(1, n_events):
        sums_copy(0, j, mine).start()
    lax.fori_loop(1, n_shells, start_sums, 0)
    sums_in[mine] = sums_out[shell]
    for j in range(1, n_events):
        sums_copy(0, j, sums_from(0, j)).wait_recv()
    lax.fori_loop(1, n_shells, wait_sums, 0)

    total = jnp.sum(sums_in[...], axis=0)
    fitted[shell] = total[0:1, :] / (total[1:2, :] + 1.0)

    def fitted_copy(i, source):
        return pltpu.make_async_remote_copy(
            src_ref=fitted.at[source],
            dst_ref=fitted.at[source],
            send_sem=send_c.at[i],
            recv_sem=recv_c.at[source],
            device_id=(event, after(shell, i, n_shells)),
            device_id_type=MESH,
        )

    def start_fitted(i, carry):
        fitted_copy(i, shell).start()
        return carry

    def wait_fitted(i, carry):
        fitted_copy(i, before(shell, i, n_shells)).wait_recv()
        return carry

    lax.fori_loop(1, n_shells, start_fitted, 0)
    lax.fori_loop(1, n_shells, wait_fitted, 0)

    correction = jnp.concatenate([fitted[h] for h in range(n_high)], axis=0)
    correction_ref[...] = correction[:correction_ref.shape[0]]
    pieces = jnp.concatenate(parts_of(correction, 3), axis=0)
    wide = dot_nn(pieces, low_hot[...])
    wide = wide[:n_high] + (wide[n_high:2 * n_high] + wide[2 * n_high:])
    picked = []
    for r in range(rows):
        hit = high_id == high[r:r + 1, :]
        picked.append(
            jnp.sum(jnp.where(hit, wide[:, r * LANES:(r + 1) * LANES], 0.0), axis=0, keepdims=True)
        )
    weighted = weight * (misfit - jnp.concatenate(picked, axis=0))
    weighted_ref[...] = weighted
    resid[shell] = weighted.astype(BF16)

    def resid_copy(i, source):
        return pltpu.make_async_remote_copy(
            src_ref=resid.at[source],
            dst_ref=resid.at[source],
            send_sem=send_d.at[i],
            recv_sem=recv_d.at[source],
            device_id=(event, after(shell, i, n_shells)),
            device_id_type=MESH,
        )

    def start_resid(i, carry):
        resid_copy(i, shell).start()
        return carry

    def wait_resid(i, carry):
        resid_copy(i, before(shell, i, n_shells)).wait_recv()
        return carry

    lax.fori_loop(1, n_shells, start_resid, 0)
    lax.fori_loop(1, n_shells, wait_resid, 0)

    found = dot_nn(pick_hot_t[...], resid[...].reshape(group_rows, LANES))
    found = jnp.where(half, found, 0.0)
    slot_rows[...] = found + swap_halves(found)

    def backward_chunk(c, carry):
        for g in range(per_chunk // GROUP):
            first = pl.multiple_of(c * per_chunk + g * GROUP, GROUP)
            picked = slot_rows[pl.ds(first, GROUP), :]
            wide = jnp.concatenate(
                [jnp.where(diagonal_mask(j), picked, 0.0).astype(BF16) for j in range(GROUP // 2)],
                axis=1,
            )
            block = blocks[pl.ds(pl.multiple_of(first * PICK_BLK, GROUP * PICK_BLK), GROUP * PICK_BLK), :]
            values[pl.ds(first, GROUP), :] = dot_nn(wide, block)
        return carry

    lax.fori_loop(0, CHUNKS, backward_chunk, 0)
    terms = jnp.concatenate(parts_of(values[...], 2), axis=1)
    part = cells // CHUNKS

    def grads_copy(c):
        piece = pl.ds(c * part, part)
        return pltpu.make_async_remote_copy(
            src_ref=grads_out.at[piece, :],
            dst_ref=grads_in.at[piece, :],
            send_sem=send_e.at[c],
            recv_sem=recv_e.at[c],
            device_id=(1 - event, shell),
            device_id_type=MESH,
        )

    for c in range(CHUNKS):
        both = dot_nn(cell_hot[c * part:(c + 1) * part, :], terms)
        grads = both[:, :LANES] + both[:, LANES:]
        if n_events == 2:
            grads_out[c * part:(c + 1) * part, :] = grads.astype(BF16)
            grads_copy(c).start()
        else:
            gradient_ref[c * part:(c + 1) * part, :] = grads

    def sent(i, carry):
        partial_copy(i, shell).wait_send()
        fitted_copy(i, shell).wait_send()
        resid_copy(i, shell).wait_send()
        for j in range(n_events):
            sums_copy(i, j, mine).wait_send()
        return carry

    for j in range(1, n_events):
        sums_copy(0, j, mine).wait_send()
    lax.fori_loop(1, n_shells, sent, 0)
    if n_events == 2:
        for c in range(CHUNKS):
            grads_copy(c).wait_recv()
            piece = slice(c * part, (c + 1) * part)
            gradient_ref[piece, :] = grads_out[piece, :].astype(F32) + grads_in[piece, :].astype(F32)
        for c in range(CHUNKS):
            grads_copy(c).wait_send()


def local(n_events, n_shells, model, sensitivity, pick_block, cell_block, blk_count, observed, pick_weight, station):
    slots = sensitivity.shape[0]
    cells = model.shape[0] // CELL_BLK
    rows = observed.shape[0] // LANES
    group_rows = rows * n_shells
    high_rows = STATIONS // LANES
    n_high = max(high_rows, n_shells)
    n_devices = n_events * n_shells
    dma = lambda n: pltpu.SemaphoreType.DMA((n,))
    vmem = pl.BlockSpec(memory_space=pltpu.VMEM)
    gradient, correction, weighted = pl.pallas_call(
        functools.partial(whole_kernel, n_events, n_shells),
        out_shape=(
            jax.ShapeDtypeStruct((cells, CELL_BLK), F32),
            jax.ShapeDtypeStruct((high_rows, LANES), F32),
            jax.ShapeDtypeStruct((rows, LANES), F32),
        ),
        in_specs=[pl.BlockSpec(memory_space=pltpu.SMEM), pl.BlockSpec(memory_space=pl.ANY)]
        + [vmem] * 6,
        out_specs=(vmem,) * 3,
        scratch_shapes=[
            pltpu.VMEM((slots * PICK_BLK, CELL_BLK), BF16),
            pltpu.VMEM((group_rows, slots), BF16),
            pltpu.VMEM((slots, group_rows), BF16),
            pltpu.VMEM((cells, slots), BF16),
            pltpu.VMEM((slots, CELL_BLK), BF16),
            pltpu.VMEM((slots, LANES), F32),
            pltpu.VMEM((slots, LANES), F32),
            pltpu.VMEM((group_rows, LANES), F32),
            pltpu.VMEM((n_shells, rows, LANES), F32),
            pltpu.VMEM((LANES, rows * LANES), BF16),
            pltpu.VMEM((3 * n_high, rows * LANES), BF16),
            pltpu.VMEM((n_high, 2, LANES), F32),
            pltpu.VMEM((n_devices, 2, LANES), F32),
            pltpu.VMEM((n_high, 1, LANES), F32),
            pltpu.VMEM((n_shells, rows, LANES), BF16),
            pltpu.VMEM((cells, CELL_BLK), BF16),
            pltpu.VMEM((cells, CELL_BLK), BF16),
            dma(CHUNKS),
            dma(n_shells), dma(n_shells), dma(n_devices), dma(n_devices),
            dma(n_shells), dma(n_shells), dma(n_shells), dma(n_shells),
            dma(CHUNKS), dma(CHUNKS),
        ],
        compiler_params=pltpu.CompilerParams(
            collective_id=0, has_side_effects=True, vmem_limit_bytes=60 * 1024 * 1024
        ),
    )(
        blk_count,
        sensitivity.reshape(slots * PICK_BLK, CELL_BLK),
        model.reshape(cells, CELL_BLK),
        pick_block.reshape(1, slots),
        cell_block.reshape(1, slots),
        observed.reshape(rows, LANES),
        pick_weight.reshape(rows, LANES),
        station.reshape(rows, LANES),
    )
    if n_events != 2:
        gradient = lax.psum(gradient, "events")
    return (gradient.reshape(-1), correction.reshape(-1), weighted.reshape(-1))


def solution(mesh):
    every = P(("events", "shells"))
    placed = (P("shells"), P(("events", "shells"), None, None)) + (every,) * 6
    return jax.shard_map(
        functools.partial(local, mesh.shape["events"], mesh.shape["shells"]),
        mesh=mesh,
        in_specs=placed,
        out_specs=(P("shells"), P(), every),
        check_vma=False,
    )
```

time: 60.4 us -> 44.9 us (0.74)
  waiting for transfers between devices: 7.2 us -> 0 us
  Pallas kernels: 46 us -> 39 us
  starting transfers between devices: 1.18 us -> 0 us
  local copies, waits for them, and re-layouts: 3.48 us -> 4.29 us
  other arithmetic: 0.73 us -> 0 us
    ppermute x1 -> x0, waiting for transfers between devices: 7.2 us -> none  [local(): other = lax.ppermute(grads, 'events', [(0, 1), (1, 0)])]
    pallas_call x3 -> x1, Pallas kernels: 46 us -> 39 us  [local(): pl.pallas_call(functools.partial(whole_kernel, n_events, n_shells), out_s...]
    ppermute x1 -> x0, starting transfers between devices: 1.18 us -> none  [local(): other = lax.ppermute(grads, 'events', [(0, 1), (1, 0)])]
    unnamed x18 -> x3, local copies, waits for them, and re-layouts: 3.48 us -> 4.29 us
    reshape x1 -> x0, other arithmetic: 0.73 us -> none  [local(): return (gradient.reshape(-1), correction.reshape(-1), weighted.reshape(-1))]
  transfers between devices with their start and end apart: 1 -> 0, of which waited for: 1 -> 0; matrix products, arithmetic and copies ran while one was open for 0% -> 0% of each run, Pallas kernels for 0% -> 0%
where the time goes in v2:
time: 44.9 us; the launch traced here: 44.6 us
  Pallas kernels  39 us (87%)
  local copies, waits for them, and re-layouts  4.29 us (10%)
  between operations  1.29 us (3%)
    pallas_call x1, Pallas kernels, local(): pl.pallas_call(functools.partial(whole_kernel, n_events, n_shells), out_s...  39 us
    unnamed x3, local copies, waits for them, and re-layouts  4.29 us

profile of v2, /device:TPU:0, one launch (start us, length us, event | category | flops | bytes accessed | tf_op | source)
XLA Modules:
  0.0 44.6 jit_solution(10095908213207677521)
XLA Ops:
  1.3 39.0 %shard_map.103 = (f32[512,128]{1,0:T(8,128)}, f32[16,128]{1,0:T(8,128)}, f32[32,128]{1,0:T(8,128)}) custom-call(s32[1]{0:T(128)S(6)} %copy.14.count_ref, bf16[32768,128]{1,0:T(8,128)(2,1)} %bitcast.10, bf16[512,128]{1,0:T(8,128)(2,1)} %bitcast.12, s32[1,512]{1,0:T(1,128)} %bitcast.18, s32[1,512]{1,0:T(1,128)} %bitcast.19, f32[32,128]{1,0:T(8,128)} %bitcast.13, ...), custom_call_target="tpu_custom_call" | custom-call | tf_op jit(solution)/shard_map/pallas_call | solution.py:359
  40.3 1.7 %copy.15 = f32[65536]{0:T(1024)} copy(f32[65536]{0:T(1024)} %bitcast.11) | data formatting | bytes 524288
  42.0 1.3 %copy.16 = f32[2048]{0:T(1024)} copy(f32[2048]{0:T(1024)} %bitcast.17) | data formatting | bytes 16384
  43.3 1.3 %copy.17 = f32[4096]{0:T(1024)} copy(f32[4096]{0:T(1024)} %bitcast.16) | data formatting | bytes 32768

commit v3 on v2

--- a/solution.py
+++ b/solution.py
@@ -51,13 +51,19 @@
     return pltpu.roll(x, PICK_BLK, 1)
 
 
+def finish_kernel(own_ref, other_ref, correction_in, weighted_in, gradient_ref, correction_ref, weighted_ref):
+    gradient_ref[...] = own_ref[...].astype(F32) + other_ref[...].astype(F32)
+    correction_ref[...] = correction_in[...]
+    weighted_ref[...] = weighted_in[...]
+
+
 def whole_kernel(
     n_events, n_shells,
     count_ref, blocks_ref, model_ref, pick_ref, cell_ref, observed_ref, weight_ref, station_ref,
-    gradient_ref, correction_ref, weighted_ref,
+    grads_out, grads_in, correction_ref, weighted_ref,
     blocks, pick_hot, pick_hot_t, cell_hot, model_rows, slot_rows, values, partial, landed,
-    low_hot, spread, sums_out, sums_in, fitted, resid, grads_out, grads_in,
-    load_sem, send_a, recv_a, send_b, recv_b, send_c, recv_c, send_d, recv_d, send_e, recv_e,
+    pair_in, paired, low_hot, spread, sums_out, sums_in, fitted, resid,
+    load_sem, send_p, recv_p, send_a, recv_a, send_b, recv_b, send_c, recv_c, send_d, recv_d, send_e, recv_e,
 ):
     event = lax.axis_index("events")
     shell = lax.axis_index("shells")
@@ -112,7 +118,12 @@
         found = found + dot_nn(hot, model_ref[b * LANES:(b + 1) * LANES, :])
     model_rows[...] = found.astype(BF16)
     pick_row = lax.shift_right_arithmetic(pick, 1)
-    pick_hot[...] = one_hot(group_rows, pick_row)
+    n_chips = n_shells // 2
+    chip, core = shell // 2, lax.rem(shell, 2)
+    half_rows = group_rows // 2
+    owner = pick_row // rows
+    moved = ((owner % 2) * n_chips + owner // 2) * rows + pick_row % rows
+    pick_hot[...] = one_hot(group_rows, jnp.where(alive, moved, -1))
     cell_hot[...] = one_hot(cells, cell)
     pick_column = jnp.transpose(jnp.broadcast_to(pick, (LANES, slots)))
     half = (pick_column & 1) == lane // PICK_BLK
@@ -137,27 +148,45 @@
     lax.fori_loop(0, CHUNKS, forward_chunk, 0)
     v = values[...]
     v = jnp.where(half, v + swap_halves(v), 0.0)
-    both = dot_nn(pick_hot[...], jnp.concatenate(parts_of(v, 2), axis=1))
-    partial[...] = both[:, :LANES] + both[:, LANES:]
-
+    terms = jnp.concatenate(parts_of(v, 2), axis=1)
+
+    def sum_half(which):
+        piece = pl.ds(pl.multiple_of(which * half_rows, half_rows), half_rows)
+        both = dot_nn(pick_hot[piece, :], terms)
+        partial[piece, :] = both[:, :LANES] + both[:, LANES:]
+        return piece
+
+    sum_half_sent = sum_half(1 - core)
     pl.semaphore_wait(barrier, n_devices - 1)
+    pair_copy = pltpu.make_async_remote_copy(
+        src_ref=partial.at[sum_half_sent, :],
+        dst_ref=pair_in,
+        send_sem=send_p.at[0],
+        recv_sem=recv_p.at[0],
+        device_id=(event, shell + 1 - 2 * core),
+        device_id_type=MESH,
+    )
+    pair_copy.start()
+    kept = sum_half(core)
+    pair_copy.wait_recv()
+    paired[...] = partial[kept, :] + pair_in[...]
 
     def partial_copy(i, source):
-        other = after(shell, i, n_shells)
+        other = after(chip, i, n_chips)
         return pltpu.make_async_remote_copy(
-            src_ref=partial.at[pl.ds(pl.multiple_of(other * rows, rows), rows), :],
+            src_ref=paired.at[pl.ds(pl.multiple_of(other * rows, rows), rows), :],
             dst_ref=landed.at[source],
             send_sem=send_a.at[i],
             recv_sem=recv_a.at[source],
-            device_id=(event, other),
+            device_id=(event, other * 2 + core),
             device_id_type=MESH,
         )
 
     def start_partial(i, carry):
-        partial_copy(i, shell).start()
-        return carry
-
-    lax.fori_loop(1, n_shells, start_partial, 0)
+        partial_copy(i, chip).start()
+        return carry
+
+    lax.fori_loop(1, n_chips, start_partial, 0)
 
     station = station_ref[...]
     high, low = station // LANES, lax.rem(station, LANES)
@@ -183,12 +212,12 @@
         sums_out[h, 1:2, :] = denom[h:h + 1, :]
 
     def take_partial(i, total):
-        source = before(shell, i, n_shells)
+        source = before(chip, i, n_chips)
         partial_copy(i, source).wait_recv()
         return total + landed[source]
 
-    own = partial[pl.ds(pl.multiple_of(shell * rows, rows), rows), :]
-    predicted = lax.fori_loop(1, n_shells, take_partial, own)
+    own = paired[pl.ds(pl.multiple_of(chip * rows, rows), rows), :]
+    predicted = lax.fori_loop(1, n_chips, take_partial, own)
     misfit = observed_ref[...] - predicted
     numer = station_sums(weight * misfit)
     for h in range(n_high):
@@ -324,10 +353,9 @@
             grads_out[c * part:(c + 1) * part, :] = grads.astype(BF16)
             grads_copy(c).start()
         else:
-            gradient_ref[c * part:(c + 1) * part, :] = grads
+            grads_out[c * part:(c + 1) * part, :] = grads
 
     def sent(i, carry):
-        partial_copy(i, shell).wait_send()
         fitted_copy(i, shell).wait_send()
         resid_copy(i, shell).wait_send()
         for j in range(n_events):
@@ -337,13 +365,16 @@
     for j in range(1, n_events):
         sums_copy(0, j, mine).wait_send()
     lax.fori_loop(1, n_shells, sent, 0)
+
+    def partial_sent(i, carry):
+        partial_copy(i, chip).wait_send()
+        return carry
+
+    pair_copy.wait_send()
+    lax.fori_loop(1, n_chips, partial_sent, 0)
     if n_events == 2:
         for c in range(CHUNKS):
-            grads_copy(c).wait_recv()
-            piece = slice(c * part, (c + 1) * part)
-            gradient_ref[piece, :] = grads_out[piece, :].astype(F32) + grads_in[piece, :].astype(F32)
-        for c in range(CHUNKS):
-            grads_copy(c).wait_send()
+            grads_copy(c).wait()
 
 
 def local(n_events, n_shells, model, sensitivity, pick_block, cell_block, blk_count, observed, pick_weight, station):
@@ -354,18 +385,21 @@
     high_rows = STATIONS // LANES
     n_high = max(high_rows, n_shells)
     n_devices = n_events * n_shells
+    n_chips = n_shells // 2
+    two = n_events == 2
     dma = lambda n: pltpu.SemaphoreType.DMA((n,))
     vmem = pl.BlockSpec(memory_space=pltpu.VMEM)
-    gradient, correction, weighted = pl.pallas_call(
+    own, other, correction, weighted = pl.pallas_call(
         functools.partial(whole_kernel, n_events, n_shells),
         out_shape=(
-            jax.ShapeDtypeStruct((cells, CELL_BLK), F32),
+            jax.ShapeDtypeStruct((cells, CELL_BLK), BF16 if two else F32),
+            jax.ShapeDtypeStruct((cells if two else GROUP, CELL_BLK), BF16),
             jax.ShapeDtypeStruct((high_rows, LANES), F32),
             jax.ShapeDtypeStruct((rows, LANES), F32),
         ),
         in_specs=[pl.BlockSpec(memory_space=pltpu.SMEM), pl.BlockSpec(memory_space=pl.ANY)]
         + [vmem] * 6,
-        out_specs=(vmem,) * 3,
+        out_specs=(vmem,) * 4,
         scratch_shapes=[
             pltpu.VMEM((slots * PICK_BLK, CELL_BLK), BF16),
             pltpu.VMEM((group_rows, slots), BF16),
@@ -375,17 +409,17 @@
             pltpu.VMEM((slots, LANES), F32),
             pltpu.VMEM((slots, LANES), F32),
             pltpu.VMEM((group_rows, LANES), F32),
-            pltpu.VMEM((n_shells, rows, LANES), F32),
+            pltpu.VMEM((n_chips, rows, LANES), F32),
+            pltpu.VMEM((group_rows // 2, LANES), F32),
+            pltpu.VMEM((group_rows // 2, LANES), F32),
             pltpu.VMEM((LANES, rows * LANES), BF16),
             pltpu.VMEM((3 * n_high, rows * LANES), BF16),
             pltpu.VMEM((n_high, 2, LANES), F32),
             pltpu.VMEM((n_devices, 2, LANES), F32),
             pltpu.VMEM((n_high, 1, LANES), F32),
             pltpu.VMEM((n_shells, rows, LANES), BF16),
-            pltpu.VMEM((cells, CELL_BLK), BF16),
-            pltpu.VMEM((cells, CELL_BLK), BF16),
-            dma(CHUNKS),
-            dma(n_shells), dma(n_shells), dma(n_devices), dma(n_devices),
+            dma(CHUNKS), dma(1), dma(1),
+            dma(n_chips), dma(n_chips), dma(n_devices), dma(n_devices),
             dma(n_shells), dma(n_shells), dma(n_shells), dma(n_shells),
             dma(CHUNKS), dma(CHUNKS),
         ],
@@ -402,8 +436,20 @@
         pick_weight.reshape(rows, LANES),
         station.reshape(rows, LANES),
     )
-    if n_events != 2:
-        gradient = lax.psum(gradient, "events")
+    if two:
+        gradient, correction, weighted = pl.pallas_call(
+            finish_kernel,
+            out_shape=(
+                jax.ShapeDtypeStruct((cells, CELL_BLK), F32),
+                jax.ShapeDtypeStruct((high_rows, LANES), F32),
+                jax.ShapeDtypeStruct((rows, LANES), F32),
+            ),
+            in_specs=[vmem] * 4,
+            out_specs=(vmem,) * 3,
+            compiler_params=pltpu.CompilerParams(vmem_limit_bytes=60 * 1024 * 1024),
+        )(own, other, correction, weighted)
+    else:
+        gradient = lax.psum(own, "events")
     return (gradient.reshape(-1), correction.reshape(-1), weighted.reshape(-1))
 
 

time: 44.9 us -> 40.5 us (0.902)
  local copies, waits for them, and re-layouts: 4.29 us -> 0 us
    unnamed x3 -> x0, local copies, waits for them, and re-layouts: 4.29 us -> none
    pallas_call x0 -> x1, Pallas kernels: none -> 1.71 us  [local(): pl.pallas_call(finish_kernel, out_shape=(jax.ShapeDtypeStruct((cells, CEL...]
    pallas_call x1, Pallas kernels: 39 us -> 37.3 us  [local(): pl.pallas_call(functools.partial(whole_kernel, n_events, n_shells), out_s...]
where the time goes in v3:
time: 40.5 us; the launch traced here: 40.3 us
  Pallas kernels  39 us (96%)
  between operations  1.29 us (3%)
    pallas_call x1, Pallas kernels, local(): pl.pallas_call(functools.partial(whole_kernel, n_events, n_shells), out_s...  37.3 us
    pallas_call x1, Pallas kernels, local(): pl.pallas_call(finish_kernel, out_shape=(jax.ShapeDtypeStruct((cells, CEL...  1.71 us

profile of v3, /device:TPU:0, one launch (start us, length us, event | category | flops | bytes accessed | tf_op | source)
XLA Modules:
  0.0 40.3 jit_solution(5883453308353351559)
XLA Ops:
  1.3 37.3 %shard_map.103 = (bf16[512,128]{1,0:T(8,128)(2,1)}, bf16[512,128]{1,0:T(8,128)(2,1)}, f32[16,128]{1,0:T(8,128)}, f32[32,128]{1,0:T(8,128)}) custom-call(s32[1]{0:T(128)S(6)} %copy.11.count_ref, bf16[32768,128]{1,0:T(8,128)(2,1)} %bitcast.10, bf16[512,128]{1,0:T(8,128)(2,1)} %bitcast.11, s32[1,512]{1,0:T(1,128)} %bitcast.15, s32[1,512]{1,0:T(1,128)} %bitcast.16, ...), custom_call_target="tpu_custom_call" | custom-call | tf_op jit(solution)/shard_map/pallas_call | solution.py:392
  38.6 1.7 %shard_map.104 = (f32[512,128]{1,0:T(8,128)}, f32[16,128]{1,0:T(8,128)}, f32[32,128]{1,0:T(8,128)}) custom-call(bf16[512,128]{1,0:T(8,128)(2,1)} %get-tuple-element.10.own_ref, bf16[512,128]{1,0:T(8,128)(2,1)} %get-tuple-element.11.other_ref, f32[16,128]{1,0:T(8,128)} %get-tuple-element.12.correction_in, f32[32,128]{1,0:T(8,128)} %get-tuple-element.13.weighted_in), custom_call_target="tpu_custom_call" | custom-call | tf_op jit(solution)/shard_map/pallas_call | solution.py:440

commit v4 on v3

--- a/solution.py
+++ b/solution.py
@@ -63,7 +63,7 @@
     grads_out, grads_in, correction_ref, weighted_ref,
     blocks, pick_hot, pick_hot_t, cell_hot, model_rows, slot_rows, values, partial, landed,
     pair_in, paired, low_hot, spread, sums_out, sums_in, fitted, resid,
-    load_sem, send_p, recv_p, send_a, recv_a, send_b, recv_b, send_c, recv_c, send_d, recv_d, send_e, recv_e,
+    load_sem, send_p, recv_p, send_a, recv_a, send_b, recv_b, send_c, recv_c, send_d, recv_d, send_f, recv_f, send_e, recv_e,
 ):
     event = lax.axis_index("events")
     shell = lax.axis_index("shells")
@@ -195,16 +195,16 @@
     high_id = lax.broadcasted_iota(jnp.int32, (n_high, LANES), 0)
 
     def station_sums(x):
-        pieces = parts_of(x, 3)
+        pieces = parts_of(x, 2)
         for r in range(rows):
             hit = high_id == high[r:r + 1, :]
-            for k in range(3):
+            for k in range(2):
                 piece = pieces[k][r:r + 1, :].astype(F32)
                 spread[k * n_high:(k + 1) * n_high, r * LANES:(r + 1) * LANES] = jnp.where(
                     hit, piece, 0.0
                 ).astype(BF16)
         out = dot_nt(spread[...], low_hot[...])
-        return out[:n_high] + (out[n_high:2 * n_high] + out[2 * n_high:])
+        return out[:n_high] + out[n_high:]
 
     weight = weight_ref[...]
     denom = station_sums(weight)
@@ -281,9 +281,9 @@
 
     correction = jnp.concatenate([fitted[h] for h in range(n_high)], axis=0)
     correction_ref[...] = correction[:correction_ref.shape[0]]
-    pieces = jnp.concatenate(parts_of(correction, 3), axis=0)
+    pieces = jnp.concatenate(parts_of(correction, 2), axis=0)
     wide = dot_nn(pieces, low_hot[...])
-    wide = wide[:n_high] + (wide[n_high:2 * n_high] + wide[2 * n_high:])
+    wide = wide[:n_high] + wide[n_high:]
     picked = []
     for r in range(rows):
         hit = high_id == high[r:r + 1, :]
@@ -299,8 +299,18 @@
             src_ref=resid.at[source],
             dst_ref=resid.at[source],
             send_sem=send_d.at[i],
-            recv_sem=recv_d.at[source],
-            device_id=(event, after(shell, i, n_shells)),
+            recv_sem=recv_d.at[i],
+            device_id=(event, after(chip, i, n_chips) * 2 + core),
+            device_id_type=MESH,
+        )
+
+    def shared_copy(i, source):
+        return pltpu.make_async_remote_copy(
+            src_ref=resid.at[source],
+            dst_ref=resid.at[source],
+            send_sem=send_f.at[i],
+            recv_sem=recv_f.at[i],
+            device_id=(event, shell + 1 - 2 * core),
             device_id_type=MESH,
         )
 
@@ -308,12 +318,20 @@
         resid_copy(i, shell).start()
         return carry
 
+    def share_resid(i, carry):
+        source = before(chip, i, n_chips) * 2 + core
+        resid_copy(i, source).wait_recv()
+        shared_copy(i, source).start()
+        return carry
+
     def wait_resid(i, carry):
-        resid_copy(i, before(shell, i, n_shells)).wait_recv()
-        return carry
-
-    lax.fori_loop(1, n_shells, start_resid, 0)
-    lax.fori_loop(1, n_shells, wait_resid, 0)
+        shared_copy(i, before(chip, i, n_chips) * 2 + 1 - core).wait_recv()
+        return carry
+
+    lax.fori_loop(1, n_chips, start_resid, 0)
+    shared_copy(0, shell).start()
+    lax.fori_loop(1, n_chips, share_resid, 0)
+    lax.fori_loop(0, n_chips, wait_resid, 0)
 
     found = dot_nn(pick_hot_t[...], resid[...].reshape(group_rows, LANES))
     found = jnp.where(half, found, 0.0)
@@ -357,7 +375,6 @@
 
     def sent(i, carry):
         fitted_copy(i, shell).wait_send()
-        resid_copy(i, shell).wait_send()
         for j in range(n_events):
             sums_copy(i, j, mine).wait_send()
         return carry
@@ -368,9 +385,12 @@
 
     def partial_sent(i, carry):
         partial_copy(i, chip).wait_send()
+        resid_copy(i, shell).wait_send()
+        shared_copy(i, before(chip, i, n_chips) * 2 + core).wait_send()
         return carry
 
     pair_copy.wait_send()
+    shared_copy(0, shell).wait_send()
     lax.fori_loop(1, n_chips, partial_sent, 0)
     if n_events == 2:
         for c in range(CHUNKS):
@@ -413,14 +433,14 @@
             pltpu.VMEM((group_rows // 2, LANES), F32),
             pltpu.VMEM((group_rows // 2, LANES), F32),
             pltpu.VMEM((LANES, rows * LANES), BF16),
-            pltpu.VMEM((3 * n_high, rows * LANES), BF16),
+            pltpu.VMEM((2 * n_high, rows * LANES), BF16),
             pltpu.VMEM((n_high, 2, LANES), F32),
             pltpu.VMEM((n_devices, 2, LANES), F32),
             pltpu.VMEM((n_high, 1, LANES), F32),
             pltpu.VMEM((n_shells, rows, LANES), BF16),
             dma(CHUNKS), dma(1), dma(1),
             dma(n_chips), dma(n_chips), dma(n_devices), dma(n_devices),
-            dma(n_shells), dma(n_shells), dma(n_shells), dma(n_shells),
+            dma(n_shells), dma(n_shells), dma(n_chips), dma(n_chips), dma(n_chips), dma(n_chips),
             dma(CHUNKS), dma(CHUNKS),
         ],
         compiler_params=pltpu.CompilerParams(

time: 40.5 us -> 40.6 us (level)
  no operation moved by 1% of the time
where the time goes in v4:
time: 40.6 us; the launch traced here: 40.4 us
  Pallas kernels  39.1 us (96%)
  between operations  1.29 us (3%)
    pallas_call x1, Pallas kernels, local(): pl.pallas_call(functools.partial(whole_kernel, n_events, n_shells), out_s...  37.4 us
    pallas_call x1, Pallas kernels, local(): pl.pallas_call(finish_kernel, out_shape=(jax.ShapeDtypeStruct((cells, CEL...  1.71 us

profile of v4, /device:TPU:0, one launch (start us, length us, event | category | flops | bytes accessed | tf_op | source)
XLA Modules:
  0.0 40.4 jit_solution(2828957745588844319)
XLA Ops:
  1.3 37.4 %shard_map.103 = (bf16[512,128]{1,0:T(8,128)(2,1)}, bf16[512,128]{1,0:T(8,128)(2,1)}, f32[16,128]{1,0:T(8,128)}, f32[32,128]{1,0:T(8,128)}) custom-call(s32[1]{0:T(128)S(6)} %copy.11.count_ref, bf16[32768,128]{1,0:T(8,128)(2,1)} %bitcast.10, bf16[512,128]{1,0:T(8,128)(2,1)} %bitcast.11, s32[1,512]{1,0:T(1,128)} %bitcast.15, s32[1,512]{1,0:T(1,128)} %bitcast.16, ...), custom_call_target="tpu_custom_call" | custom-call | tf_op jit(solution)/shard_map/pallas_call | solution.py:412
  38.7 1.7 %shard_map.104 = (f32[512,128]{1,0:T(8,128)}, f32[16,128]{1,0:T(8,128)}, f32[32,128]{1,0:T(8,128)}) custom-call(bf16[512,128]{1,0:T(8,128)(2,1)} %get-tuple-element.10.own_ref, bf16[512,128]{1,0:T(8,128)(2,1)} %get-tuple-element.11.other_ref, f32[16,128]{1,0:T(8,128)} %get-tuple-element.12.correction_in, f32[32,128]{1,0:T(8,128)} %get-tuple-element.13.weighted_in), custom_call_target="tpu_custom_call" | custom-call | tf_op jit(solution)/shard_map/pallas_call | solution.py:460

commit v5 on v3

--- a/solution.py
+++ b/solution.py
@@ -124,7 +124,6 @@
     owner = pick_row // rows
     moved = ((owner % 2) * n_chips + owner // 2) * rows + pick_row % rows
     pick_hot[...] = one_hot(group_rows, jnp.where(alive, moved, -1))
-    cell_hot[...] = one_hot(cells, cell)
     pick_column = jnp.transpose(jnp.broadcast_to(pick, (LANES, slots)))
     half = (pick_column & 1) == lane // PICK_BLK
     pick_column = lax.shift_right_arithmetic(pick_column, 1)
@@ -195,16 +194,16 @@
     high_id = lax.broadcasted_iota(jnp.int32, (n_high, LANES), 0)
 
     def station_sums(x):
-        pieces = parts_of(x, 3)
+        pieces = parts_of(x, 2)
         for r in range(rows):
             hit = high_id == high[r:r + 1, :]
-            for k in range(3):
+            for k in range(2):
                 piece = pieces[k][r:r + 1, :].astype(F32)
                 spread[k * n_high:(k + 1) * n_high, r * LANES:(r + 1) * LANES] = jnp.where(
                     hit, piece, 0.0
                 ).astype(BF16)
         out = dot_nt(spread[...], low_hot[...])
-        return out[:n_high] + (out[n_high:2 * n_high] + out[2 * n_high:])
+        return out[:n_high] + out[n_high:]
 
     weight = weight_ref[...]
     denom = station_sums(weight)
@@ -281,9 +280,9 @@
 
     correction = jnp.concatenate([fitted[h] for h in range(n_high)], axis=0)
     correction_ref[...] = correction[:correction_ref.shape[0]]
-    pieces = jnp.concatenate(parts_of(correction, 3), axis=0)
+    pieces = jnp.concatenate(parts_of(correction, 2), axis=0)
     wide = dot_nn(pieces, low_hot[...])
-    wide = wide[:n_high] + (wide[n_high:2 * n_high] + wide[2 * n_high:])
+    wide = wide[:n_high] + wide[n_high:]
     picked = []
     for r in range(rows):
         hit = high_id == high[r:r + 1, :]
@@ -313,6 +312,7 @@
         return carry
 
     lax.fori_loop(1, n_shells, start_resid, 0)
+    cell_hot[...] = one_hot(cells, cell)
     lax.fori_loop(1, n_shells, wait_resid, 0)
 
     found = dot_nn(pick_hot_t[...], resid[...].reshape(group_rows, LANES))
@@ -413,7 +413,7 @@
             pltpu.VMEM((group_rows // 2, LANES), F32),
             pltpu.VMEM((group_rows // 2, LANES), F32),
             pltpu.VMEM((LANES, rows * LANES), BF16),
-            pltpu.VMEM((3 * n_high, rows * LANES), BF16),
+            pltpu.VMEM((2 * n_high, rows * LANES), BF16),
             pltpu.VMEM((n_high, 2, LANES), F32),
             pltpu.VMEM((n_devices, 2, LANES), F32),
             pltpu.VMEM((n_high, 1, LANES), F32),

time: 40.5 us -> 40.5 us (level)
  no operation moved by 1% of the time
where the time goes in v5:
time: 40.5 us; the launch traced here: 40.3 us
  Pallas kernels  39 us (96%)
  between operations  1.29 us (3%)
    pallas_call x1, Pallas kernels, local(): pl.pallas_call(functools.partial(whole_kernel, n_events, n_shells), out_s...  37.3 us
    pallas_call x1, Pallas kernels, local(): pl.pallas_call(finish_kernel, out_shape=(jax.ShapeDtypeStruct((cells, CEL...  1.71 us

profile of v5, /device:TPU:0, one launch (start us, length us, event | category | flops | bytes accessed | tf_op | source)
XLA Modules:
  0.0 40.3 jit_solution(4087102048369201115)
XLA Ops:
  1.3 37.3 %shard_map.103 = (bf16[512,128]{1,0:T(8,128)(2,1)}, bf16[512,128]{1,0:T(8,128)(2,1)}, f32[16,128]{1,0:T(8,128)}, f32[32,128]{1,0:T(8,128)}) custom-call(s32[1]{0:T(128)S(6)} %copy.11.count_ref, bf16[32768,128]{1,0:T(8,128)(2,1)} %bitcast.10, bf16[512,128]{1,0:T(8,128)(2,1)} %bitcast.11, s32[1,512]{1,0:T(1,128)} %bitcast.15, s32[1,512]{1,0:T(1,128)} %bitcast.16, ...), custom_call_target="tpu_custom_call" | custom-call | tf_op jit(solution)/shard_map/pallas_call | solution.py:392
  38.6 1.7 %shard_map.104 = (f32[512,128]{1,0:T(8,128)}, f32[16,128]{1,0:T(8,128)}, f32[32,128]{1,0:T(8,128)}) custom-call(bf16[512,128]{1,0:T(8,128)(2,1)} %get-tuple-element.10.own_ref, bf16[512,128]{1,0:T(8,128)(2,1)} %get-tuple-element.11.other_ref, f32[16,128]{1,0:T(8,128)} %get-tuple-element.12.correction_in, f32[32,128]{1,0:T(8,128)} %get-tuple-element.13.weighted_in), custom_call_target="tpu_custom_call" | custom-call | tf_op jit(solution)/shard_map/pallas_call | solution.py:440
